TPU v7x, 512 devices: a whole 4x4x16 slice. The times are simulated.
512 devices in a mesh: dp: 32 (over x, z_lo), expert: 16 (over y, z_hi, core).
Axes of the slice: x: 4, y: 4, z: 16 (z_hi: 2, z_lo: 8; z = z_hi * 8 + z_lo), core: 2. Of those that a mesh axis runs over, the one named last changes fastest.
Arguments:
- grads: bfloat16 [262144, 768], P(('dp', 'expert'))
- block_expert: int32 [8192], P(('dp', 'expert')), may hold values from 0 to 15, as said below
- grad_weight: bfloat16 [16, 4096, 768], P('expert', 'dp'), may hold values from -1.1953125 to 1.1953125
- damping: float32 [16], P('expert'), may hold values from 0.1 to 1
Outputs:
- preconditioned: float32 [16, 4096, 768], P('expert', 'dp')
Inputs may be any that keep to these rules, and one draw needn't show every extreme that they name: `block_expert`: among the 16 blocks of one device no expert appears more than 2 times; in every draw one expert appears exactly 2 times on every device.
All inputs are finite; a program needn't handle non-finite values.
Results may differ from a plain program's by a relative error of at most 0.0003.
Values may be sent and summed in bfloat16 or wider, within the bound.
No kernel may reach another device: no remote copies, remote signals or barrier semaphores. Data moves between devices by JAX's collectives and lax.ppermute only.
A program may use at most 128 MiB of HBM per device.

v0:
```python
import jax
import jax.numpy as jnp
from jax import lax
from jax.sharding import PartitionSpec as P

EXP_DEV = 1
FB = 128


def from_root(value, axis, source):
    kept = jnp.where(lax.axis_index(axis) == source, value, 0).astype(value.dtype)
    return lax.psum(kept, axis)


def product(left, right):
    return jnp.dot(left, right, precision=lax.Precision.HIGHEST)


def tri_index(row_block, col_block):
    return row_block * (row_block + 1) // 2 + col_block


def lower_inverse_blocks(packed, scale, damp, block_count):
    identity = jnp.eye(FB, dtype=jnp.float32)

    def entry(row_block, col_block):
        value = packed[tri_index(row_block, col_block)] * scale
        if row_block == col_block:
            value = value + damp * identity
        return value

    lower = {}
    diag_inv = {}
    for step in range(block_count):
        acc = entry(step, step)
        for other in range(step):
            acc = acc - product(lower[step, other], lower[step, other].T)
        lower[step, step] = jnp.linalg.cholesky(acc)
        diag_inv[step] = jax.scipy.linalg.solve_triangular(lower[step, step], identity, lower=True)
        for row_block in range(step + 1, block_count):
            acc = entry(row_block, step)
            for other in range(step):
                acc = acc - product(lower[row_block, other], lower[step, other].T)
            lower[row_block, step] = product(acc, diag_inv[step].T)
    inverse_blocks = {}
    for col_block in range(block_count):
        inverse_blocks[col_block, col_block] = diag_inv[col_block]
        for row_block in range(col_block + 1, block_count):
            total = jnp.zeros((FB, FB), jnp.float32)
            for other in range(col_block, row_block):
                total = total + product(lower[row_block, other], inverse_blocks[other, col_block])
            inverse_blocks[row_block, col_block] = -product(diag_inv[row_block], total)
    return inverse_blocks


def pack_blocks(blocks, block_count):
    return jnp.stack(
        [
            blocks[upper, lower_idx]
            for upper in range(block_count)
            for lower_idx in range(upper + 1)
        ],
        axis=0,
    )


def unpack_triangle(packed, block_count):
    rows_list = []
    for upper in range(block_count):
        pieces = []
        for lower_idx in range(block_count):
            if lower_idx <= upper:
                pieces.append(packed[tri_index(upper, lower_idx)])
            else:
                pieces.append(jnp.zeros((FB, FB), jnp.float32))
        rows_list.append(jnp.concatenate(pieces, axis=1))
    return jnp.concatenate(rows_list, axis=0)


def full_inverse(packed, scale, damp, block_count):
    blocks = lower_inverse_blocks(packed, scale, damp, block_count)
    lower_inv = unpack_triangle(pack_blocks(blocks, block_count), block_count)
    return product(lower_inv.T, lower_inv)


def block_gram(received):
    return jnp.einsum("skrf,skrg->kfg", received, received, preferred_element_type=jnp.float32)


def shards(grads, block_expert, grad_weight, damping):
    group_count = lax.axis_size("expert")
    data_count = lax.axis_size("dp")
    token_count, feature_count = grads.shape
    block_total = block_expert.shape[0]
    block_rows = token_count // block_total
    expert_total = EXP_DEV * group_count
    capacity = max(2, (2 * block_total + expert_total - 1) // expert_total)
    same_expert = block_expert[:, None] == block_expert[None, :]
    position = jnp.arange(block_total, dtype=jnp.int32)
    earlier = position[None, :] < position[:, None]
    rank = jnp.sum(jnp.where(same_expert & earlier, 1, 0), axis=1).astype(jnp.int32)
    target_slot = block_expert * capacity + rank
    slot_ids = jnp.arange(expert_total * capacity, dtype=jnp.int32)
    placement = (slot_ids[:, None] == target_slot[None, :]).astype(jnp.bfloat16)
    flat_blocks = grads.reshape(block_total, block_rows * feature_count)
    sectioned = jnp.dot(placement, flat_blocks, preferred_element_type=jnp.float32).astype(
        jnp.bfloat16
    )
    sectioned = sectioned.reshape(group_count, EXP_DEV, capacity * block_rows, feature_count)
    grams = block_gram(lax.all_to_all(sectioned, "expert", split_axis=0, concat_axis=0, tiled=True))
    block_count = feature_count // FB
    packed = jnp.stack(
        [
            grams[0, upper * FB : (upper + 1) * FB, lower_idx * FB : (lower_idx + 1) * FB]
            for upper in range(block_count)
            for lower_idx in range(upper + 1)
        ],
        axis=0,
    )
    scale = expert_total / (token_count * data_count * group_count)
    damp = damping[0]
    weight = grad_weight[0].astype(jnp.float32)
    summed = lax.psum(packed, "dp")
    root = lax.axis_index("expert") % data_count

    def owner_full(value):
        return full_inverse(value, scale, damp, block_count)

    def other_full(value):
        return jnp.zeros((feature_count, feature_count), jnp.float32)

    inverse = lax.cond(lax.axis_index("dp") == root, owner_full, other_full, summed)
    inverse = jax.tree.map(lambda part: from_root(part, "dp", root), inverse)
    return product(weight, inverse)[None]


def solution(mesh):
    return jax.shard_map(
        shards,
        mesh=mesh,
        in_specs=(
            P(("dp", "expert"), None),
            P(("dp", "expert")),
            P("expert", "dp", None),
            P("expert"),
        ),
        out_specs=P("expert", "dp", None),
        check_vma=False,
    )
```

profile of v0, /device:TPU:24, one launch (start us, length us, event | category | flops | bytes accessed | tf_op | source)
XLA Modules:
  0.0 1208.7 jit_solution(10481540624647924509)
XLA Ops:
  6.5 0.0 copy-start
  6.5 0.0 all-reduce.3.cloned.1.call-start
  6.5 0.9 select_reduce_fusion.6
  7.5 0.7 multiply_add_fusion
  8.1 1.5 reshape.64
  9.6 0.5 convolution_convert_fusion
  10.2 0.8 reshape.65
  10.9 56.4 %all_to_all.5 = bf16[16,1,64,768]{3,2,1,0:T(8,128)(2,1)S(1)} all-to-all(bf16[16,1,64,768]{3,2,1,0:T(8,128)(2,1)S(1)} %bitcast.349), channel_id=1, replica_groups=mesh['dp'=32,'expert'=16] {'expert'}, dimensions={0} | all-to-all | bytes 3145728 | tf_op jit(solution)/shard_map/all_to_all | solution.py:110
  67.3 1.4 convolution_bitcast_fusion
  69.0 0.0 copy-start.1
  69.1 1.1 copy-done.1
  70.2 0.0 all-reduce.3.cloned.1.call-update
  70.2 0.0 all-reduce.5.cloned.1.call-start
  70.2 486.5 %all-reduce.3.cloned.1.call-done = f32[21,128,128]{2,1,0:T(8,128)} async-done(((f32[21,128,128]{2,1,0:T(8,128)}), f32[21,128,128]{2,1,0:T(8,128)}) %all-reduce.3.cloned.1.call-update) | async-done | bytes 1376272 | tf_op jit(solution)/shard_map/psum | solution.py:123
  556.7 0.4 conditional.1
  556.7 0.2 broadcast.75
  557.1 1.5 broadcast_select_fusion
  558.7 0.0 all-reduce.5.cloned.1.call-update
  558.7 638.6 %all-reduce.5.cloned.1.call-done = f32[768,768]{1,0:T(8,128)} async-done(((f32[768,768]{1,0:T(8,128)}), f32[768,768]{1,0:T(8,128)}) %all-reduce.5.cloned.1.call-update) | async-done | bytes 2359312 | tf_op jit(solution)/shard_map/psum | solution.py:12
  1197.3 0.0 copy-done
  1197.3 3.7 convolution_bitcast_fusion.1
  1201.0 0.9 copy.96
  (21 shorter events, 0.1 us)
Async XLA Ops:
  6.5 1190.7 %copy-start = (bf16[1,128,768]{2,1,0:T(8,128)(2,1)S(1)}, bf16[1,128,768]{2,1,0:T(8,128)(2,1)}, u32[]{:S(2)}) copy-start(bf16[1,128,768]{2,1,0:T(8,128)(2,1)} %param.11) | copy-start | bytes 589828
  6.5 550.2 %all-reduce.3.cloned.1.call-start = ((), (), s32[]{:S(2)}) async-start(), calls=%async_computation.1 | async-start | bytes 2752512 | tf_op jit(solution)/shard_map/psum | solution.py:123
  69.0 1.1 copy-start.1
  70.2 1127.1 %all-reduce.5.cloned.1.call-start = ((), (), s32[]{:S(2)}) async-start(), calls=%async_computation.2 | async-start | bytes 4718592 | tf_op jit(solution)/shard_map/psum | solution.py:12
Sparse Core Ops, SparseCore 0:
  70.3 486.3 all-reduce.2
  559.9 637.3 all-reduce.4
where the time goes:
time: 1210 us
  waiting for transfers between devices  1130 us (93%)
  blocking collectives  56.4 us (5%)
  between operations  13.6 us (1%)
    psum x1, waiting for transfers between devices, from_root(): return lax.psum(kept, axis)  639 us
    psum x1, waiting for transfers between devices, shards(): summed = lax.psum(packed, 'dp')  486 us
    all_to_all x1, blocking collectives, shards(): lax.all_to_all(sectioned, 'expert', split_axis=0, concat_axis=0, tiled=True)  56.4 us
  transfers between devices with their start and end apart: 2, of which 2 were waited for; matrix products, arithmetic and copies ran while one was open for 0% of the time, Pallas kernels for 0%

commit v1 on v0

v1 whole, which is shorter than its diff:
```python
import functools

import jax
import jax.numpy as jnp
from jax import lax
from jax.experimental import pallas as pl
from jax.experimental.pallas import tpu as pltpu
from jax.sharding import Mesh
from jax.sharding import PartitionSpec as P

FB = 128
FF = 768
NB = FF // FB
TRI = NB * (NB + 1) // 2
CAP = 2
CHUNK = 48
ROWS = 64 * CHUNK
BF16 = jnp.bfloat16
F32 = jnp.float32


def product(left, right):
    return jnp.dot(left, right, precision=lax.Precision.HIGHEST)


def tri_index(row_block, col_block):
    return row_block * (row_block + 1) // 2 + col_block


def lower_inverse_blocks(packed, scale, damp):
    identity = jnp.eye(FB, dtype=F32)

    def entry(row_block, col_block):
        value = packed[tri_index(row_block, col_block)] * scale
        if row_block == col_block:
            value = value + damp * identity
        return value

    lower = {}
    diag_inv = {}
    for step in range(NB):
        acc = entry(step, step)
        for other in range(step):
            acc = acc - product(lower[step, other], lower[step, other].T)
        lower[step, step] = jnp.linalg.cholesky(acc)
        diag_inv[step] = jax.scipy.linalg.solve_triangular(lower[step, step], identity, lower=True)
        for row_block in range(step + 1, NB):
            acc = entry(row_block, step)
            for other in range(step):
                acc = acc - product(lower[row_block, other], lower[step, other].T)
            lower[row_block, step] = product(acc, diag_inv[step].T)
    inverse_blocks = {}
    for col_block in range(NB):
        inverse_blocks[col_block, col_block] = diag_inv[col_block]
        for row_block in range(col_block + 1, NB):
            total = jnp.zeros((FB, FB), F32)
            for other in range(col_block, row_block):
                total = total + product(lower[row_block, other], inverse_blocks[other, col_block])
            inverse_blocks[row_block, col_block] = -product(diag_inv[row_block], total)
    return inverse_blocks


def direct_apply(packed, weight, scale, damp):
    blocks = lower_inverse_blocks(packed, scale, damp)
    rows = []
    for upper in range(NB):
        pieces = [
            blocks[upper, low] if low <= upper else jnp.zeros((FB, FB), F32) for low in range(NB)
        ]
        rows.append(jnp.concatenate(pieces, axis=1))
    lower_inv = jnp.concatenate(rows, axis=0)
    return product(weight.astype(F32), product(lower_inv.T, lower_inv))


def dot32(left, right):
    return jnp.dot(left, right, preferred_element_type=F32)


def split(value):
    high = value.astype(BF16)
    return high, (value - high.astype(F32)).astype(BF16)


def solve_kernel(scale, damp_ref, packed_ref, weight_ref, out_ref, ok_ref,
                 fh, fl, r1, r2, r4, r8, bvec, xvec):
    damp = damp_ref[0]
    row_id = lax.broadcasted_iota(jnp.int32, (FB, FB), 0)
    col_id = lax.broadcasted_iota(jnp.int32, (FB, FB), 1)
    eye = jnp.where(row_id == col_id, 1.0, 0.0).astype(F32)

    s_row, s_col = [], []
    for i in range(NB):
        t = tri_index(i, i)
        dia = packed_ref[t * FB:(t + 1) * FB, :] * eye
        s_row.append(lax.rsqrt(jnp.sum(dia, axis=0, keepdims=True) * scale + damp))
        s_col.append(lax.rsqrt(jnp.sum(dia, axis=1, keepdims=True) * scale + damp))
    norm = jnp.zeros((FB, FB), F32)
    for i in range(NB):
        for j in range(i + 1):
            t = tri_index(i, j)
            block = packed_ref[t * FB:(t + 1) * FB, :] * scale
            if i == j:
                block = block + damp * eye
            block = block * s_col[i] * s_row[j]
            norm = norm + block * block * (1.0 if i == j else 2.0)
            high, low = split(block)
            fh[i * FB:(i + 1) * FB, j * FB:(j + 1) * FB] = high
            fl[i * FB:(i + 1) * FB, j * FB:(j + 1) * FB] = low
            if i != j:
                turned = block.T
                high, low = split(turned)
                fh[j * FB:(j + 1) * FB, i * FB:(i + 1) * FB] = high
                fl[j * FB:(j + 1) * FB, i * FB:(i + 1) * FB] = low
    total = jnp.sum(jnp.sum(norm, axis=0, keepdims=True), axis=1, keepdims=True)
    alpha = float(FF) / total
    for i in range(NB):
        rows = slice(i * FB, (i + 1) * FB)
        for j in range(NB):
            cols = slice(j * FB, (j + 1) * FB)
            part = fh[rows, cols].astype(F32) + fl[rows, cols].astype(F32)
            value = -alpha * part
            if i == j:
                value = value + eye
            r1[rows, cols] = value.astype(BF16)
    for i in range(NB):
        rows = slice(i * FB, (i + 1) * FB)
        r2[rows, :] = dot32(r1[rows, :], r1[...]).astype(BF16)
    for i in range(NB):
        rows = slice(i * FB, (i + 1) * FB)
        r4[rows, :] = dot32(r2[rows, :], r2[...]).astype(BF16)
    power = jnp.zeros((1, FF), F32)
    for i in range(NB):
        rows = slice(i * FB, (i + 1) * FB)
        value = dot32(r4[rows, :], r4[...])
        power = power + jnp.sum(value * value, axis=0, keepdims=True)
        r8[rows, :] = value.astype(BF16)
    power = jnp.sum(power, axis=1, keepdims=True)

    scales = jnp.concatenate(s_row, axis=1)
    bvec[...] = weight_ref[...].astype(F32) * scales

    def near_inverse(value):
        value = value + dot32(value.astype(BF16), r8[...])
        value = value + dot32(value.astype(BF16), r4[...])
        value = value + dot32(value.astype(BF16), r2[...])
        value = value + dot32(value.astype(BF16), r1[...])
        return value * alpha

    def residual(value):
        high, low = split(value)
        return bvec[...] - (
            dot32(high, fh[...]) + (dot32(low, fh[...]) + dot32(high, fl[...]))
        )

    xvec[...] = near_inverse(bvec[...])
    xvec[...] = xvec[...] + near_inverse(residual(xvec[...]))
    left = residual(xvec[...])
    left_norm = jnp.sum(left * left, axis=1, keepdims=True)
    b_norm = jnp.sum(bvec[...] * bvec[...], axis=1, keepdims=True)
    out_ref[...] = (xvec[...] + near_inverse(left)) * scales
    bad = jnp.sum(jnp.where(left_norm <= 1e-6 * b_norm, 0.0, 1.0), axis=0, keepdims=True)
    bad = bad + jnp.where(power <= 0.25, 0.0, 1.0)
    ok_ref[...] = jnp.broadcast_to(bad, (8, 128))


def refined_apply(packed, weight, scale, damp):
    return pl.pallas_call(
        functools.partial(solve_kernel, scale),
        out_shape=(
            jax.ShapeDtypeStruct((FB, FF), F32),
            jax.ShapeDtypeStruct((8, 128), F32),
        ),
        in_specs=[
            pl.BlockSpec(memory_space=pltpu.SMEM),
            pl.BlockSpec(memory_space=pltpu.VMEM),
            pl.BlockSpec(memory_space=pltpu.VMEM),
        ],
        out_specs=(
            pl.BlockSpec(memory_space=pltpu.VMEM),
            pl.BlockSpec(memory_space=pltpu.VMEM),
        ),
        scratch_shapes=[pltpu.VMEM((FF, FF), BF16)] * 6 + [pltpu.VMEM((FB, FF), F32)] * 2,
        compiler_params=pltpu.CompilerParams(vmem_limit_bytes=40 * 1024 * 1024),
    )(damp, packed, weight)


def exchange(value, axis):
    return lax.all_to_all(value, axis, split_axis=0, concat_axis=0, tiled=True)


def gather(value, axis, count):
    return exchange(jnp.broadcast_to(value[None], (count,) + value.shape), axis)


def shards(grads, block_expert, grad_weight, damping):
    token_count = grads.shape[0]
    block_total = block_expert.shape[0]
    block_rows = token_count // block_total
    expert_total = 16
    scale = expert_total / (token_count * 512.0)

    same_expert = block_expert[:, None] == block_expert[None, :]
    position = jnp.arange(block_total, dtype=jnp.int32)
    earlier = position[None, :] < position[:, None]
    rank = jnp.sum(jnp.where(same_expert & earlier, 1, 0), axis=1).astype(jnp.int32)
    target = (block_expert % 4) * 4 + block_expert // 4
    slot = target * CAP + rank
    slot_ids = jnp.arange(expert_total * CAP, dtype=jnp.int32)
    placement = (slot_ids[:, None] == slot[None, :]).astype(BF16)
    flat = grads.reshape(block_total, block_rows * FF)
    routed = jnp.dot(placement, flat, preferred_element_type=F32).astype(BF16)
    routed = exchange(routed.reshape(expert_total, CAP * block_rows, FF), ("x", "y"))
    tokens = routed.reshape(-1, FF)
    gram = lax.dot_general(tokens, tokens, (((0,), (0,)), ((), ())), preferred_element_type=F32)

    blocks = [
        gram[i * FB:(i + 1) * FB, j * FB:(j + 1) * FB] for i in range(NB) for j in range(i + 1)
    ]
    packed = jnp.concatenate(blocks + [jnp.zeros((ROWS - TRI * FB, FB), F32)], axis=0)
    packed = packed.reshape(32, 2, CHUNK, FB).transpose(1, 0, 2, 3)
    packed = jnp.sum(exchange(packed, "core"), axis=0)
    packed = exchange(packed, ("x", "zl")).reshape(4, 8, CHUNK, FB).sum(1)
    packed = exchange(packed, ("zh", "core")).reshape(2, 2 * CHUNK, FB).sum(0)
    packed = gather(packed, "zl", 8).reshape(16 * CHUNK, FB)
    packed = gather(packed, "x", 4).reshape(ROWS, FB)

    weight = grad_weight[0]
    result, bad = refined_apply(packed, weight, scale, damping)

    def keep(_):
        return result

    def direct(_):
        return direct_apply(packed[:TRI * FB].reshape(TRI, FB, FB), weight, scale, damping[0])

    return lax.cond(bad[0, 0] == 0.0, keep, direct, 0)[None]


def solution(mesh):
    fine = Mesh(mesh.devices.reshape(4, 8, 4, 2, 2), ("x", "zl", "y", "zh", "core"))
    every = ("x", "zl", "y", "zh", "core")
    return jax.shard_map(
        shards,
        mesh=fine,
        in_specs=(
            P(every, None),
            P(every),
            P(("y", "zh", "core"), ("x", "zl"), None),
            P(("y", "zh", "core")),
        ),
        out_specs=P(("y", "zh", "core"), ("x", "zl"), None),
        check_vma=False,
    )
```

time: 1210 us -> 364 us (0.30)
  the two profiles are of different devices: /device:TPU:24 before, /device:TPU:32 now
where the time goes in v1:
time: 364 us; the launch traced here: 360 us
  other arithmetic  140 us (38%)
  blocking collectives  136 us (37%)
  matrix products  42.4 us (12%)
  waiting for transfers between devices  18.9 us (5%)
  Pallas kernels  9.18 us (3%)
  local copies, waits for them, and re-layouts  6.4 us (2%)
  starting transfers between devices  4.09 us (1%)
    all_to_all x5, blocking collectives, exchange(): return lax.all_to_all(value, axis, split_axis=0, concat_axis=0, tiled=True)  136 us
    another operation x18, other arithmetic, lower_inverse_blocks(): lower[step, step] = jnp.linalg.cholesky(acc)  74.4 us
    another operation x12, other arithmetic, lower_inverse_blocks(): jax.scipy.linalg.solve_triangular(lower[step, step], identity, lower=True)  62.5 us
    dot_general x102, matrix products, product(): return jnp.dot(left, right, precision=lax.Precision.HIGHEST)  39.2 us
    all_to_all x1, waiting for transfers between devices, exchange(): return lax.all_to_all(value, axis, split_axis=0, concat_axis=0, tiled=True)  18.9 us
    pallas_call x1, Pallas kernels, refined_apply(): pl.pallas_call(functools.partial(solve_kernel, scale), out_shape=(jax.Sha...  9.18 us
  transfers between devices with their start and end apart: 1, of which 1 were waited for; matrix products, arithmetic and copies ran while one was open for 0% of the time, Pallas kernels for 0%

profile of v1, /device:TPU:32, one launch (start us, length us, event | category | flops | bytes accessed | tf_op | source)
XLA Modules:
  0.0 359.7 jit_solution(4827158000843545620)
XLA Ops:
  0.0 0.9 select_reduce_fusion.6
  0.9 0.7 multiply_add_fusion
  1.6 1.5 reshape.79
  3.6 0.8 reshape.80
  4.4 29.4 %all_to_all.30 = bf16[16,64,768]{2,1,0:T(8,128)(2,1)S(1)} all-to-all(bf16[16,64,768]{2,1,0:T(8,128)(2,1)S(1)} %reshape.80), channel_id=1, replica_groups=mesh['x'=4,'zl'=8,'y'=4,'zh'=2,'core'=2] {'x','y'}, dimensions={0} | all-to-all | bytes 3145728 | tf_op jit(solution)/shard_map/all_to_all | solution.py:188
  33.8 1.4 convolution_bitcast_fusion.1
  35.7 5.0 %all_to_all.31 = f32[2,32,48,128]{3,2,1,0:T(8,128)S(1)} all-to-all(f32[2,32,48,128]{3,2,1,0:T(8,128)S(1)} %copy.141), channel_id=1, replica_groups=mesh['x'=4,'zl'=8,'y'=4,'zh'=2,'core'=2] {'core'}, dimensions={0} | all-to-all | bytes 3145728 | tf_op jit(solution)/shard_map/all_to_all | solution.py:188
  40.8 54.3 %all_to_all.32 = f32[32,48,128]{2,1,0:T(8,128)S(1)} all-to-all(f32[32,48,128]{2,1,0:T(8,128)S(1)} %reduce_sum.37), channel_id=1, replica_groups=mesh['x'=4,'zl'=8,'y'=4,'zh'=2,'core'=2] {'x','zl'}, dimensions={0} | all-to-all | bytes 1572864 | tf_op jit(solution)/shard_map/all_to_all | solution.py:188
  95.2 22.5 %all_to_all.33 = f32[4,48,128]{2,1,0:T(8,128)S(1)} all-to-all(f32[4,48,128]{2,1,0:T(8,128)S(1)} %bitcast_reduce_fusion), channel_id=1, replica_groups=mesh['x'=4,'zl'=8,'y'=4,'zh'=2,'core'=2] {'zh','core'}, dimensions={0} | all-to-all | bytes 196608 | tf_op jit(solution)/shard_map/all_to_all | solution.py:188
  117.7 24.4 %all_to_all.34 = f32[8,96,128]{2,1,0:T(8,128)S(1)} all-to-all(f32[8,96,128]{2,1,0:T(8,128)S(1)} %broadcast_in_dim.41), channel_id=1, replica_groups=mesh['x'=4,'zl'=8,'y'=4,'zh'=2,'core'=2] {'zl'}, dimensions={0} | all-to-all | bytes 786432 | tf_op jit(solution)/shard_map/all_to_all | solution.py:188
  142.1 1.3 broadcast_in_dim.43
  143.4 4.1 %all-to-all-start.5 = ((f32[4,768,128]{2,1,0:T(8,128)}), f32[4,768,128]{2,1,0:T(8,128)S(1)}, u32[]{:S(2)}, u32[]{:S(2)}) async-start(f32[4,768,128]{2,1,0:T(8,128)} %broadcast_in_dim.43), calls=%async_computation.5 | async-start | bytes 3145728 | tf_op jit(solution)/shard_map/all_to_all | solution.py:188
  148.1 18.9 %all-to-all-done.5 = f32[4,768,128]{2,1,0:T(8,128)S(1)} async-done(((f32[4,768,128]{2,1,0:T(8,128)}), f32[4,768,128]{2,1,0:T(8,128)S(1)}, u32[]{:S(2)}, u32[]{:S(2)}) %all-to-all-start.5) | async-done | bytes 1572896 | tf_op jit(solution)/shard_map/all_to_all | solution.py:188
  167.0 9.2 %shard_map.48 = (f32[128,768]{1,0:T(8,128)}, f32[8,128]{1,0:T(8,128)S(1)}) custom-call(f32[1]{0:T(128)S(6)} %copy.227.damp_ref, f32[3072,128]{1,0:T(8,128)S(1)} %bitcast.276, bf16[128,768]{1,0:T(8,128)(2,1)S(1)} %bitcast.281), custom_call_target="tpu_custom_call" | custom-call | tf_op jit(solution)/shard_map/pallas_call | solution.py:167
  176.2 0.6 slice.199
  177.4 181.2 %conditional.1 = (f32[1,128,768]{2,1,0:T(8,128)S(1)}) conditional(s32[]{:T(128)} %bitcast.30, (f32[3072,128]{1,0:T(8,128)S(1)}, f32[1]{0:T(128)}, bf16[128,768]{1,0:T(8,128)(2,1)S(1)}) %tuple.36, f32[128,768]{1,0:T(8,128)} %get-tuple-element.25), branch_computations={%region_4.9_spmd, %region_7.10_spmd} | conditional | flops 9012691968 | bytes 41687092 | solution.py:236
  178.1 0.7 select_add_fusion.5
  178.9 0.7 fusion.39
  179.5 11.7 %cholesky.104 = f32[128,128]{1,0:T(8,128)S(1)} custom-call(f32[128,128]{1,0:T(8,128)S(1)} %fusion.39), custom_call_target="Cholesky" | custom-call | tf_op jit(solution)/shard_map/cond/branch_0_fun/jit(cholesky)/cholesky | solution.py:45
  191.3 0.6 compare_reduce_fusion.5
  191.9 0.6 fusion.17
  192.5 9.8 %custom-call.10 = f32[1,128,128]{1,2,0:T(8,128)S(1)} custom-call(f32[1,128,128]{2,1,0:T(8,128)S(1)} %fusion.17), custom_call_target="InvertDiagBlocksLowerTriangular" | custom-call | tf_op jit(solution)/shard_map/cond/branch_0_fun/jit(_solve_triangular)/triangular_solve | solution.py:46
  204.0 0.9 convolution_subtract_fusion.34
  205.0 11.7 %cholesky.115 = f32[128,128]{1,0:T(8,128)S(1)} custom-call(f32[128,128]{1,0:T(8,128)S(1)} %fusion.37), custom_call_target="Cholesky" | custom-call | tf_op jit(solution)/shard_map/cond/branch_0_fun/jit(cholesky)/cholesky | solution.py:45
  216.8 0.6 compare_reduce_fusion.4
  217.4 0.6 fusion.18
  218.0 10.0 %custom-call.11 = f32[1,128,128]{1,2,0:T(8,128)S(1)} custom-call(f32[1,128,128]{2,1,0:T(8,128)S(1)} %fusion.18), custom_call_target="InvertDiagBlocksLowerTriangular" | custom-call | tf_op jit(solution)/shard_map/cond/branch_0_fun/jit(_solve_triangular)/triangular_solve | solution.py:46
  234.0 0.9 convolution_subtract_fusion.33
  235.5 11.7 %cholesky.126 = f32[128,128]{1,0:T(8,128)S(1)} custom-call(f32[128,128]{1,0:T(8,128)S(1)} %fusion.35), custom_call_target="Cholesky" | custom-call | tf_op jit(solution)/shard_map/cond/branch_0_fun/jit(cholesky)/cholesky | solution.py:45
  247.3 0.6 compare_reduce_fusion.3
  247.9 0.6 fusion.19
  248.5 9.8 %custom-call.12 = f32[1,128,128]{1,2,0:T(8,128)S(1)} custom-call(f32[1,128,128]{2,1,0:T(8,128)S(1)} %fusion.19), custom_call_target="InvertDiagBlocksLowerTriangular" | custom-call | tf_op jit(solution)/shard_map/cond/branch_0_fun/jit(_solve_triangular)/triangular_solve | solution.py:46
  259.4 0.6 fusion.62
  262.5 0.9 convolution_subtract_fusion.30
  264.3 11.7 %cholesky.137 = f32[128,128]{1,0:T(8,128)S(1)} custom-call(f32[128,128]{1,0:T(8,128)S(1)} %fusion.33), custom_call_target="Cholesky" | custom-call | tf_op jit(solution)/shard_map/cond/branch_0_fun/jit(cholesky)/cholesky | solution.py:45
  276.1 0.6 compare_reduce_fusion.2
  277.3 9.8 %custom-call.13 = f32[1,128,128]{1,2,0:T(8,128)S(1)} custom-call(f32[1,128,128]{2,1,0:T(8,128)S(1)} %fusion.20), custom_call_target="InvertDiagBlocksLowerTriangular" | custom-call | tf_op jit(solution)/shard_map/cond/branch_0_fun/jit(_solve_triangular)/triangular_solve | solution.py:46
  289.8 0.9 convolution_subtract_fusion.24
  290.7 0.9 convolution_subtract_fusion.14
  294.2 11.9 %cholesky.148 = f32[128,128]{1,0:T(8,128)S(1)} custom-call(f32[128,128]{1,0:T(8,128)S(1)} %fusion.31), custom_call_target="Cholesky" | custom-call | tf_op jit(solution)/shard_map/cond/branch_0_fun/jit(cholesky)/cholesky | solution.py:45
  306.1 0.6 compare_reduce_fusion.1
  307.3 9.8 %custom-call.14 = f32[1,128,128]{1,2,0:T(8,128)S(1)} custom-call(f32[1,128,128]{2,1,0:T(8,128)S(1)} %fusion.21), custom_call_target="InvertDiagBlocksLowerTriangular" | custom-call | tf_op jit(solution)/shard_map/cond/branch_0_fun/jit(_solve_triangular)/triangular_solve | solution.py:46
  318.0 11.7 %cholesky.159 = f32[128,128]{1,0:T(8,128)S(1)} custom-call(f32[128,128]{1,0:T(8,128)S(1)} %fusion.29), custom_call_target="Cholesky" | custom-call | tf_op jit(solution)/shard_map/cond/branch_0_fun/jit(cholesky)/cholesky | solution.py:45
  329.7 0.6 compare_reduce_fusion
  331.0 9.8 %custom-call.15 = f32[1,128,128]{1,2,0:T(8,128)S(1)} custom-call(f32[1,128,128]{2,1,0:T(8,128)S(1)} %fusion.22), custom_call_target="InvertDiagBlocksLowerTriangular" | custom-call | tf_op jit(solution)/shard_map/cond/branch_0_fun/jit(_solve_triangular)/triangular_solve | solution.py:46
  350.1 6.0 %fusion.79 = f32[768,768]{1,0:T(8,128)S(1)} fusion(f32[768,768]{0,1:T(8,128)S(1)} %constant_dynamic-update-slice_fusion.5), kind=kOutput, calls=%fused_computation.257 | convolution fusion | flops 5435817984 | bytes 4718592 | tf_op jit(solution)/shard_map/cond/branch_0_fun/dot_general | solution.py:23
  356.1 2.0 convolution_bitcast_fusion
  358.6 0.7 copy-done.1
  (164 shorter events, 31.6 us)
Async XLA Ops:
  142.1 24.9 %copy-start = (bf16[1,128,768]{2,1,0:T(8,128)(2,1)S(1)}, bf16[1,128,768]{2,1,0:T(8,128)(2,1)}, u32[]{:S(2)}) copy-start(bf16[1,128,768]{2,1,0:T(8,128)(2,1)} %param.11) | copy-start | bytes 589828
  143.4 23.6 %all-to-all-start.5 = ((f32[4,768,128]{2,1,0:T(8,128)}), f32[4,768,128]{2,1,0:T(8,128)S(1)}, u32[]{:S(2)}, u32[]{:S(2)}) async-start(f32[4,768,128]{2,1,0:T(8,128)} %broadcast_in_dim.43), calls=%async_computation.5 | async-start | bytes 3145728 | tf_op jit(solution)/shard_map/all_to_all | solution.py:188
  358.6 0.7 copy-start.1

commit v2 on v1

v2 whole, which is shorter than its diff:
```python
import functools

import jax
import jax.numpy as jnp
from jax import lax
from jax.experimental import pallas as pl
from jax.experimental.pallas import tpu as pltpu
from jax.sharding import Mesh
from jax.sharding import PartitionSpec as P

FB = 128
FF = 768
NB = FF // FB
TRI = NB * (NB + 1) // 2
CAP = 2
TB = 32
EXPERTS = 16
PIECE = TRI * FB // 32
BF16 = jnp.bfloat16
F32 = jnp.float32


def tri_index(row_block, col_block):
    return row_block * (row_block + 1) // 2 + col_block


def dot32(left, right):
    return jnp.dot(left, right, preferred_element_type=F32)


def split(value):
    high = value.astype(BF16)
    return high, (value - high.astype(F32)).astype(BF16)


def solve_kernel(scale, damp_ref, packed_ref, weight_ref, out_ref,
                 fh, fl, r1, r2, r4, r8, bvec, xvec, full):
    damp = damp_ref[0]
    row_id = lax.broadcasted_iota(jnp.int32, (FB, FB), 0)
    col_id = lax.broadcasted_iota(jnp.int32, (FB, FB), 1)
    eye = jnp.where(row_id == col_id, 1.0, 0.0).astype(F32)

    s_row, s_col = [], []
    for i in range(NB):
        t = tri_index(i, i)
        dia = packed_ref[t * FB:(t + 1) * FB, :] * eye
        s_row.append(lax.rsqrt(jnp.sum(dia, axis=0, keepdims=True) * scale + damp))
        s_col.append(lax.rsqrt(jnp.sum(dia, axis=1, keepdims=True) * scale + damp))
    norm = jnp.zeros((FB, FB), F32)
    for i in range(NB):
        for j in range(i + 1):
            t = tri_index(i, j)
            block = packed_ref[t * FB:(t + 1) * FB, :] * scale
            if i == j:
                block = block + damp * eye
            block = block * s_col[i] * s_row[j]
            norm = norm + block * block * (1.0 if i == j else 2.0)
            high, low = split(block)
            fh[i * FB:(i + 1) * FB, j * FB:(j + 1) * FB] = high
            fl[i * FB:(i + 1) * FB, j * FB:(j + 1) * FB] = low
            if i != j:
                turned = block.T
                high, low = split(turned)
                fh[j * FB:(j + 1) * FB, i * FB:(i + 1) * FB] = high
                fl[j * FB:(j + 1) * FB, i * FB:(i + 1) * FB] = low
    total = jnp.sum(jnp.sum(norm, axis=0, keepdims=True), axis=1, keepdims=True)
    alpha = float(FF) / total
    for i in range(NB):
        rows = slice(i * FB, (i + 1) * FB)
        for j in range(NB):
            cols = slice(j * FB, (j + 1) * FB)
            part = fh[rows, cols].astype(F32) + fl[rows, cols].astype(F32)
            value = -alpha * part
            if i == j:
                value = value + eye
            r1[rows, cols] = value.astype(BF16)
    for i in range(NB):
        rows = slice(i * FB, (i + 1) * FB)
        r2[rows, :] = dot32(r1[rows, :], r1[...]).astype(BF16)
    for i in range(NB):
        rows = slice(i * FB, (i + 1) * FB)
        r4[rows, :] = dot32(r2[rows, :], r2[...]).astype(BF16)
    power = jnp.zeros((1, FF), F32)
    for i in range(NB):
        rows = slice(i * FB, (i + 1) * FB)
        value = dot32(r4[rows, :], r4[...])
        power = power + jnp.sum(value * value, axis=0, keepdims=True)
        r8[rows, :] = value.astype(BF16)
    power = jnp.sum(power, axis=1, keepdims=True)

    scales = jnp.concatenate(s_row, axis=1)
    bvec[...] = weight_ref[...].astype(F32) * scales

    def near_inverse(value):
        value = value + dot32(value.astype(BF16), r8[...])
        value = value + dot32(value.astype(BF16), r4[...])
        value = value + dot32(value.astype(BF16), r2[...])
        value = value + dot32(value.astype(BF16), r1[...])
        return value * alpha

    def residual(value):
        high, low = split(value)
        return bvec[...] - (
            dot32(high, fh[...]) + (dot32(low, fh[...]) + dot32(high, fl[...]))
        )

    xvec[...] = near_inverse(bvec[...])
    xvec[...] = xvec[...] + near_inverse(residual(xvec[...]))
    left = residual(xvec[...])
    left_norm = jnp.sum(left * left, axis=1, keepdims=True)
    b_norm = jnp.sum(bvec[...] * bvec[...], axis=1, keepdims=True)
    out_ref[...] = (xvec[...] + near_inverse(left)) * scales
    bad = jnp.sum(jnp.where(left_norm <= 1e-6 * b_norm, 0.0, 1.0), axis=0, keepdims=True)
    bad = bad + jnp.where(power <= 0.25, 0.0, 1.0)

    @pl.when(bad[0, 0] > 0.0)
    def _():
        direct_inverse(scale, damp, packed_ref, s_row, s_col, eye, full)
        out_ref[...] = (
            jnp.dot(bvec[...], full[...], preferred_element_type=F32, precision=lax.Precision.HIGHEST)
            * scales
        )


def direct_inverse(scale, damp, packed_ref, s_row, s_col, eye, full):
    for i in range(NB):
        for j in range(i + 1):
            t = tri_index(i, j)
            block = packed_ref[t * FB:(t + 1) * FB, :] * scale
            if i == j:
                block = block + damp * eye
            block = block * s_col[i] * s_row[j]
            full[i * FB:(i + 1) * FB, j * FB:(j + 1) * FB] = block
            if i != j:
                full[j * FB:(j + 1) * FB, i * FB:(i + 1) * FB] = block.T
    lanes = lax.broadcasted_iota(jnp.int32, (1, FF), 1)
    sublanes = lax.broadcasted_iota(jnp.int32, (FB, 1), 0)

    def step(k, carry):
        at = jnp.where(lanes == k, 1.0, 0.0)
        row = full[pl.ds(k, 1), :]
        inv = 1.0 / jnp.sum(row * at, axis=1, keepdims=True)
        scaled = row * inv
        scaled = jnp.where(lanes == k, inv, scaled)

        def part(i, inner):
            start = pl.multiple_of(i * FB, FB)
            own = full[pl.ds(start, FB), :]
            column = jnp.sum(own * at, axis=1, keepdims=True)
            rest = own * (1.0 - at) - column * scaled
            full[pl.ds(start, FB), :] = jnp.where(sublanes + start == k, scaled, rest)
            return inner

        return lax.fori_loop(0, NB, part, carry)

    lax.fori_loop(0, FF, step, 0)


def refined_apply(packed, weight, scale, damp):
    return pl.pallas_call(
        functools.partial(solve_kernel, scale),
        out_shape=jax.ShapeDtypeStruct((FB, FF), F32),
        in_specs=[
            pl.BlockSpec(memory_space=pltpu.SMEM),
            pl.BlockSpec(memory_space=pltpu.VMEM),
            pl.BlockSpec(memory_space=pltpu.VMEM),
        ],
        out_specs=pl.BlockSpec(memory_space=pltpu.VMEM),
        scratch_shapes=[pltpu.VMEM((FF, FF), BF16)] * 6
        + [pltpu.VMEM((FB, FF), F32)] * 2
        + [pltpu.VMEM((FF, FF), F32)],
        compiler_params=pltpu.CompilerParams(vmem_limit_bytes=40 * 1024 * 1024),
    )(damp, packed, weight)


def exchange(value, axis):
    return lax.all_to_all(value, axis, split_axis=0, concat_axis=0, tiled=True)


def gather(value, axis, count):
    return exchange(jnp.broadcast_to(value[None], (count,) + value.shape), axis)


def route_kernel(expert_ref, grads_ref, out_ref, seen):
    for e in range(EXPERTS):
        seen[e] = 0
    out_ref[...] = jnp.zeros_like(out_ref)
    for b in range(grads_ref.shape[0] // TB):
        expert = expert_ref[b]
        rank = seen[expert]
        seen[expert] = rank + 1
        target = (expert % 4) * 4 + expert // 4
        start = pl.multiple_of((target * CAP + rank) * TB, TB)
        out_ref[pl.ds(start, TB), :] = grads_ref[b * TB:(b + 1) * TB, :]


def route(grads, block_expert):
    return pl.pallas_call(
        route_kernel,
        out_shape=jax.ShapeDtypeStruct((EXPERTS * CAP * TB, FF), BF16),
        in_specs=[
            pl.BlockSpec(memory_space=pltpu.SMEM),
            pl.BlockSpec(memory_space=pltpu.VMEM),
        ],
        out_specs=pl.BlockSpec(memory_space=pltpu.VMEM),
        scratch_shapes=[pltpu.SMEM((EXPERTS,), jnp.int32)],
        compiler_params=pltpu.CompilerParams(vmem_limit_bytes=16 * 1024 * 1024),
    )(block_expert, grads)


def shards(grads, block_expert, grad_weight, damping):
    scale = EXPERTS / (grads.shape[0] * 512.0)
    routed = route(grads, block_expert).reshape(EXPERTS, CAP * TB, FF)
    tokens = exchange(routed, ("x", "y")).reshape(-1, FF)
    gram = lax.dot_general(tokens, tokens, (((0,), (0,)), ((), ())), preferred_element_type=F32)

    blocks = [
        gram[i * FB:(i + 1) * FB, j * FB:(j + 1) * FB] for i in range(NB) for j in range(i + 1)
    ]
    packed = jnp.concatenate(blocks, axis=0)
    packed = packed.reshape(16, 2, PIECE, FB).transpose(1, 0, 2, 3)
    packed = jnp.sum(exchange(packed, "core"), axis=0)
    packed = exchange(packed, ("x", "zb")).reshape(4, 4, PIECE, FB).sum(1)
    packed = jnp.broadcast_to(packed[None], (2, 4, PIECE, FB)).reshape(8, PIECE, FB)
    packed = exchange(packed, ("za", "zh", "core")).reshape(4, 2 * PIECE, FB).sum(0)
    packed = gather(packed, "zb", 4).reshape(8 * PIECE, FB)
    packed = gather(packed, "x", 4).reshape(32 * PIECE, FB)
    return refined_apply(packed, grad_weight[0], scale, damping)[None]


def solution(mesh):
    every = ("x", "za", "zb", "y", "zh", "core")
    fine = Mesh(mesh.devices.reshape(4, 2, 4, 4, 2, 2), every)
    experts, rows = ("y", "zh", "core"), ("x", "za", "zb")
    return jax.shard_map(
        shards,
        mesh=fine,
        in_specs=(P(every, None), P(every), P(experts, rows, None), P(experts)),
        out_specs=P(experts, rows, None),
        check_vma=False,
    )
```

time: 364 us -> 826 us (2.27)
  the two profiles are of different devices: /device:TPU:32 before, /device:TPU:24 now
where the time goes in v2:
time: 826 us; the launch traced here: 825 us
  Pallas kernels  689 us (83%)
  blocking collectives  109 us (13%)
  waiting for transfers between devices  16 us (2%)
    pallas_call x1, Pallas kernels, refined_apply(): pl.pallas_call(functools.partial(solve_kernel, scale), out_shape=jax.Shap...  688 us
    all_to_all x5, blocking collectives, exchange(): return lax.all_to_all(value, axis, split_axis=0, concat_axis=0, tiled=True)  109 us
  transfers between devices with their start and end apart: 1, of which 1 were waited for; matrix products, arithmetic and copies ran while one was open for 0% of the time, Pallas kernels for 0%

profile of v2, /device:TPU:24, one launch (start us, length us, event | category | flops | bytes accessed | tf_op | source)
XLA Modules:
  0.0 824.5 jit_solution(903134001755357064)
XLA Ops:
  0.0 0.0 copy-start
  0.0 1.1 copy-done
  1.1 0.0 copy-start.2
  1.1 0.7 copy-done.2
  1.8 0.7 shard_map.46
  2.5 27.1 %all_to_all.30 = bf16[16,64,768]{2,1,0:T(8,128)(2,1)S(1)} all-to-all(bf16[16,64,768]{2,1,0:T(8,128)(2,1)S(1)} %bitcast.13), channel_id=1, replica_groups=mesh['x'=4,'za'=2,'zb'=4,'y'=4,'zh'=2,'core'=2] {'x','y'}, dimensions={0} | all-to-all | bytes 3145728 | tf_op jit(solution)/shard_map/all_to_all | solution.py:177
  29.6 1.4 convolution_bitcast_fusion
  31.4 0.1 reshape.23
  31.5 0.4 copy.7
  31.9 4.8 all_to_all.31
  36.8 0.1 reduce_sum.27
  36.9 0.2 copy.8
  37.1 27.9 %all_to_all.32 = f32[16,84,128]{2,1,0:T(8,128)S(1)} all-to-all(f32[16,84,128]{2,1,0:T(8,128)S(1)} %copy.8), channel_id=1, replica_groups=mesh['x'=4,'za'=2,'zb'=4,'y'=4,'zh'=2,'core'=2] {'x','zb'}, dimensions={0} | all-to-all | bytes 1376256 | tf_op jit(solution)/shard_map/all_to_all | solution.py:177
  65.2 34.6 %all_to_all.33 = f32[8,84,128]{2,1,0:T(8,128)S(1)} all-to-all(f32[8,84,128]{2,1,0:T(8,128)S(1)} %bitcast.17), channel_id=1, replica_groups=mesh['x'=4,'za'=2,'zb'=4,'y'=4,'zh'=2,'core'=2] {'za','zh','core'}, dimensions={0} | all-to-all | bytes 688128 | tf_op jit(solution)/shard_map/all_to_all | solution.py:177
  99.9 14.9 %all_to_all.34 = f32[4,168,128]{2,1,0:T(8,128)S(1)} all-to-all(f32[4,168,128]{2,1,0:T(8,128)S(1)} %broadcast_in_dim.11), channel_id=1, replica_groups=mesh['x'=4,'za'=2,'zb'=4,'y'=4,'zh'=2,'core'=2] {'zb'}, dimensions={0} | all-to-all | bytes 688128 | tf_op jit(solution)/shard_map/all_to_all | solution.py:177
  114.8 1.2 broadcast_in_dim.25
  115.9 0.0 copy-start.1
  115.9 3.7 all-to-all-start.5
  120.3 16.0 %all-to-all-done.5 = f32[4,672,128]{2,1,0:T(8,128)S(1)} async-done(((f32[4,672,128]{2,1,0:T(8,128)}), f32[4,672,128]{2,1,0:T(8,128)S(1)}, u32[]{:S(2)}, u32[]{:S(2)}) %all-to-all-start.5) | async-done | bytes 1376288 | tf_op jit(solution)/shard_map/all_to_all | solution.py:177
  136.3 0.0 copy-done.1
  136.3 688.2 %shard_map.47 = f32[128,768]{1,0:T(8,128)} custom-call(f32[1]{0:T(128)S(6)} %copy.31.damp_ref, f32[2688,128]{1,0:T(8,128)S(1)} %bitcast.14, bf16[128,768]{1,0:T(8,128)(2,1)S(1)} %bitcast.15), custom_call_target="tpu_custom_call" | custom-call | tf_op jit(solution)/shard_map/pallas_call | solution.py:160
  (25 shorter events, 0.3 us)
Async XLA Ops:
  0.0 1.1 copy-start
  1.1 0.7 copy-start.2
  115.9 20.4 %copy-start.1 = (bf16[1,128,768]{2,1,0:T(8,128)(2,1)S(1)}, bf16[1,128,768]{2,1,0:T(8,128)(2,1)}, u32[]{:S(2)}) copy-start(bf16[1,128,768]{2,1,0:T(8,128)(2,1)} %param.6) | copy-start | bytes 589828
  115.9 20.4 %all-to-all-start.5 = ((f32[4,672,128]{2,1,0:T(8,128)}), f32[4,672,128]{2,1,0:T(8,128)S(1)}, u32[]{:S(2)}, u32[]{:S(2)}) async-start(f32[4,672,128]{2,1,0:T(8,128)} %broadcast_in_dim.25), calls=%async_computation.5 | async-start | bytes 2752512 | tf_op jit(solution)/shard_map/all_to_all | solution.py:177
